TPU v7x, 32 devices: a whole 2x2x4 slice. The times are simulated.
32 devices in a mesh: seq: 32 (over z, y, x, core), head: 1.
Axes of the slice: x: 2, y: 2, z: 4, core: 2. Of those that a mesh axis runs over, the one named last changes fastest.
Arguments:
- query_rows: bfloat16 [4096, 2048], P('seq', 'head'), may hold values from -6 to 6
- key_rows: bfloat16 [4096, 2048], P('seq', 'head'), may hold values from -6 to 6
- value_rows: bfloat16 [4096, 2048], P('seq', 'head'), may hold values from -6 to 6
- doc_lengths: int32 [32], replicated, may hold values from 1 to 1920, 4096 in all
- norm_gain: float32 [128], replicated, may hold values from 0.25 to 1.75
- out_weight: bfloat16 [2048, 2048], P('head'), may hold values from -0.125 to 0.125
Outputs:
- layer_out: bfloat16 [4096, 2048], P('seq', 'head')
Inputs may be any that keep to these rules, and one draw needn't show every extreme that they name: `doc_lengths`: positive lengths summing to 4096; the longest has exactly 1920 tokens.
All inputs are finite; a program needn't handle non-finite values.
Results may differ from a plain program's by a relative error of at most 0.0049.
Values sent between devices are 32-bit elements; how exact they have to be, the bound alone decides.
No kernel may reach another device: no remote copies, remote signals or barrier semaphores. Data moves between devices by JAX's collectives and lax.ppermute only.
A program may use at most 320 MiB of HBM per device.

v0:
```python
import jax
import jax.numpy as jnp
from jax import lax
from jax.sharding import PartitionSpec as P

HEAD_DIM = 128
ITERS = 4
SPAN = 15


epsilon = 1e-06
damping = 1.0
highest = lax.Precision.HIGHEST


def shifted(block, axis, distance):
    devices = range(lax.axis_size(axis))
    route = [(i - distance, i) for i in devices if i - distance in devices]
    return lax.ppermute(block, axis, route)


def unit_rows(matrix_rows):
    matrix_rows = matrix_rows.astype(jnp.float32)
    return matrix_rows * lax.rsqrt(
        jnp.sum(matrix_rows * matrix_rows, axis=-1, keepdims=True) + epsilon
    )


def document_ids(doc_lengths, positions):
    starts = jnp.cumsum(doc_lengths, dtype=jnp.int32) - doc_lengths
    below = (starts[None, :] <= positions[:, None]).astype(jnp.int32)
    return jnp.sum(below, axis=1, dtype=jnp.int32) - 1


def apply_state(vector, prefix_state, carried, mask, key_block, target):
    from_prefix = (
        jnp.einsum("htj,hij->hti", vector, prefix_state, precision=highest) * carried[None, :, None]
    )
    scores = jnp.einsum("htj,hsj->hts", vector, key_block, precision=highest) * mask[None]
    return from_prefix + jnp.einsum("hts,hsi->hti", scores, target, precision=highest)


def solve_block(queries, key_block, value_block, gram, cross, carried, mask):
    solution = jnp.zeros_like(queries)
    residual = queries
    direction = queries
    norm_now = jnp.sum(residual * residual, axis=-1, keepdims=True)
    for iteration in range(ITERS):
        product_image = (
            apply_state(direction, gram, carried, mask, key_block, key_block) + damping * direction
        )
        step_size = norm_now / (
            jnp.sum(direction * product_image, axis=-1, keepdims=True) + epsilon
        )
        solution = solution + step_size * direction
        residual = residual - step_size * product_image
        norm_next = jnp.sum(residual * residual, axis=-1, keepdims=True)
        direction = residual + norm_next / (norm_now + epsilon) * direction
        norm_now = norm_next
    return apply_state(solution, cross, carried, mask, key_block, value_block)


def combine_states(earlier, latter):
    carry_on = (1 - latter[2]).astype(jnp.float32)
    return (
        latter[0] + carry_on * earlier[0],
        latter[1] + carry_on * earlier[1],
        jnp.maximum(earlier[2], latter[2]),
    )


def on_device(query_rows, key_rows, value_rows, doc_lengths, norm_gain, out_weight):
    tokens_here = query_rows.shape[0]
    heads_here = query_rows.shape[1] // HEAD_DIM

    def heads_first(matrix_rows):
        return matrix_rows.reshape(tokens_here, heads_here, HEAD_DIM).transpose(1, 0, 2)

    queries = unit_rows(heads_first(query_rows))
    keys_here = unit_rows(heads_first(key_rows))
    values = heads_first(value_rows).astype(jnp.float32)
    shard_index = lax.axis_index("seq")
    offsets = jnp.arange(tokens_here, dtype=jnp.int32)
    positions = shard_index * tokens_here + offsets
    doc_ids = document_ids(doc_lengths, positions)
    previous = document_ids(doc_lengths, positions[:1] - 1)[0]
    carried = (doc_ids == previous).astype(jnp.float32)
    restart = (doc_ids[-1] != previous).astype(jnp.int32)
    tail_mask = (doc_ids == doc_ids[-1]).astype(jnp.float32)
    tail_gram = jnp.einsum(
        "hsi,hsj->hij", keys_here * tail_mask[None, :, None], keys_here, precision=highest
    )
    tail_cross = jnp.einsum(
        "hsi,hsj->hij", values * tail_mask[None, :, None], keys_here, precision=highest
    )
    partial_value = shifted((tail_gram, tail_cross, restart), "seq", 1)
    for degree in range(SPAN.bit_length()):
        earlier = shifted((partial_value[0], partial_value[1], partial_value[2]), "seq", 2**degree)
        partial_value = combine_states(earlier, partial_value)
    gram, cross, unused = partial_value
    causal = offsets[None, :] <= offsets[:, None]
    mask = ((doc_ids[:, None] == doc_ids[None, :]) & causal).astype(jnp.float32)
    mixed_heads = solve_block(queries, keys_here, values, gram, cross, carried, mask)
    inverse_rms = lax.rsqrt(jnp.mean(mixed_heads * mixed_heads, axis=-1, keepdims=True) + epsilon)
    normed = (mixed_heads * inverse_rms * norm_gain).astype(jnp.bfloat16)
    normed = normed.transpose(1, 0, 2).reshape(tokens_here, heads_here * HEAD_DIM)
    partial_out = jnp.dot(normed, out_weight, preferred_element_type=jnp.float32)
    return lax.psum_scatter(partial_out, "head", scatter_dimension=1, tiled=True).astype(
        jnp.bfloat16
    )


def solution(mesh):
    in_specs = (P("seq", "head"), P("seq", "head"), P("seq", "head"), P(), P(), P("head", None))
    out_specs = P("seq", "head")
    return jax.shard_map(
        on_device, mesh=mesh, in_specs=in_specs, out_specs=out_specs, check_vma=False
    )
```

profile of v0, /device:TPU:0, one launch (start us, length us, event | category | flops | bytes accessed | tf_op | source)
XLA Modules:
  0.0 237.8 jit_solution(9106864034764661847)
XLA Ops:
  5.7 3.3 %fusion = f32[16,128,128]{2,1,0:T(8,128)} fusion(f32[128]{0:T(128)S(1)} %get-tuple-element.12, f32[16,128,128]{1,2,0:T(8,128)S(1)} %bitcast.64, f32[16,128]{1,0:T(8,128)S(1)} %add_rsqrt_fusion), kind=kOutput, calls=%fused_computation.2 | convolution fusion | flops 403439616 | bytes 2105856 | tf_op jit(solution)/shard_map/hsi,hsj->hij/dot_general | solution.py:90
  9.0 2.4 %collective-permute-start = (f32[16,128,128]{2,1,0:T(8,128)}, f32[16,128,128]{2,1,0:T(8,128)S(1)}, u32[]{:S(2)}, u32[]{:S(2)}) collective-permute-start(f32[16,128,128]{2,1,0:T(8,128)} %fusion), channel_id=1, source_target_pairs={{0,1},{1,2},{2,3},{3,4},{4,5},{5,6},{6,7},{7,8},{8,9},{9,10},{10,1... | collective-permute-start | bytes 3145736 | tf_op jit(solution)/shard_map/ppermute | solution.py:19
  12.7 3.3 %fusion.15 = f32[16,128,128]{2,1,0:T(8,128)} fusion(bf16[16,128,128]{1,2,0:T(8,128)(2,1)S(1)} %bitcast.79, f32[128]{0:T(128)S(1)} %get-tuple-element.12, f32[16,128,128]{1,2,0:T(8,128)S(1)} %bitcast.65, f32[16,128]{1,0:T(8,128)S(1)} %add_rsqrt_fusion), kind=kOutput, calls=%fused_computation.32 | convolution fusion | flops 403439616 | bytes 2630144 | tf_op jit(solution)/shard_map/hsi,hsj->hij/dot_general | solution.py:93
  16.0 5.4 %collective-permute-start.9 = (f32[16,128,128]{2,1,0:T(8,128)}, f32[16,128,128]{2,1,0:T(8,128)}, u32[]{:S(2)}, u32[]{:S(2)}) collective-permute-start(f32[16,128,128]{2,1,0:T(8,128)} %fusion.15), channel_id=1, source_target_pairs={{0,1},{1,2},{2,3},{3,4},{4,5},{5,6},{6,7},{7,8},{8,9},{9,10},{10,1... | collective-permute-start | bytes 3145736 | tf_op jit(solution)/shard_map/ppermute | solution.py:19
  21.4 7.4 %collective-permute-start.2 = (f32[16,128,128]{2,1,0:T(8,128)S(1)}, f32[16,128,128]{2,1,0:T(8,128)}, u32[]{:S(2)}, u32[]{:S(2)}) collective-permute-start(f32[16,128,128]{2,1,0:T(8,128)S(1)} %collective-permute-done), channel_id=1, source_target_pairs={{0,1},{1,2},{2,3},{3,4},{4,5},{5,6},{6,7},{7,8},{8,9},{9,10},{10,1... | collective-permute-start | bytes 3145736 | tf_op jit(solution)/shard_map/ppermute | solution.py:19
  29.5 4.2 %collective-permute-start.1 = (s32[]{:T(128)}, s32[]{:T(128)}, u32[]{:S(2)}, u32[]{:S(2)}) collective-permute-start(s32[]{:T(128)} %convert_element_type.80), channel_id=1, source_target_pairs={{0,1},{1,2},{2,3},{3,4},{4,5},{5,6},{6,7},{7,8},{8,9},{9,10},{10,1... | collective-permute-start | bytes 20 | tf_op jit(solution)/shard_map/ppermute | solution.py:19
  34.4 17.5 %collective-permute-start.10 = (f32[16,128,128]{2,1,0:T(8,128)}, f32[16,128,128]{2,1,0:T(8,128)}, u32[]{:S(2)}, u32[]{:S(2)}) collective-permute-start(f32[16,128,128]{2,1,0:T(8,128)} %collective-permute-done.9), channel_id=1, source_target_pairs={{0,1},{1,2},{2,3},{3,4},{4,5},{5,6},{6,7},{7,8},{8,9},{9,10},{10,1... | collective-permute-start | bytes 3145736 | tf_op jit(solution)/shard_map/ppermute | solution.py:19
  53.6 4.5 %collective-permute-start.4 = (f32[16,128,128]{2,1,0:T(8,128)S(1)}, f32[16,128,128]{2,1,0:T(8,128)}, u32[]{:S(2)}, u32[]{:S(2)}) collective-permute-start(f32[16,128,128]{2,1,0:T(8,128)S(1)} %multiply_add_fusion.10), channel_id=1, source_target_pairs={{0,2},{1,3},{2,4},{3,5},{4,6},{5,7},{6,8},{7,9},{8,10},{9,11},{10,... | collective-permute-start | bytes 3145736 | tf_op jit(solution)/shard_map/ppermute | solution.py:19
  58.1 4.6 %collective-permute-start.3 = (s32[]{:T(128)}, s32[]{:T(128)}, u32[]{:S(2)}, u32[]{:S(2)}) collective-permute-start(s32[]{:T(128)} %collective-permute-done.1), channel_id=1, source_target_pairs={{0,1},{1,2},{2,3},{3,4},{4,5},{5,6},{6,7},{7,8},{8,9},{9,10},{10,1... | collective-permute-start | bytes 20 | tf_op jit(solution)/shard_map/ppermute | solution.py:19
  64.5 2.7 %multiply_add_fusion.2 = f32[16,128,128]{2,1,0:T(8,128)} fusion(f32[16,128,128]{2,1,0:T(8,128)} %collective-permute-done.9, f32[16,128,128]{2,1,0:T(8,128)} %collective-permute-done.10, f32[]{:T(128)S(6)} %convert_element_type.81), kind=kLoop, calls=%fused_computation.31 | loop fusion | flops 524288 | bytes 3145732 | tf_op jit(solution)/shard_map/add | solution.py:67
  67.2 30.0 %collective-permute-start.11 = (f32[16,128,128]{2,1,0:T(8,128)}, f32[16,128,128]{2,1,0:T(8,128)}, u32[]{:S(2)}, u32[]{:S(2)}) collective-permute-start(f32[16,128,128]{2,1,0:T(8,128)} %multiply_add_fusion.2), channel_id=1, source_target_pairs={{0,2},{1,3},{2,4},{3,5},{4,6},{5,7},{6,8},{7,9},{8,10},{9,11},{10,... | collective-permute-start | bytes 3145736 | tf_op jit(solution)/shard_map/ppermute | solution.py:19
  97.2 2.4 %multiply_add_fusion.9 = f32[16,128,128]{2,1,0:T(8,128)} fusion(f32[16,128,128]{2,1,0:T(8,128)S(1)} %multiply_add_fusion.10, f32[16,128,128]{2,1,0:T(8,128)} %collective-permute-done.4, f32[]{:T(128)S(6)} %convert_element_type.82), kind=kLoop, calls=%fused_computation.50 | loop fusion | flops 524288 | bytes 3145732 | tf_op jit(solution)/shard_map/add | solution.py:66
  99.6 3.8 %collective-permute-start.6 = (f32[16,128,128]{2,1,0:T(8,128)}, f32[16,128,128]{2,1,0:T(8,128)}, u32[]{:S(2)}, u32[]{:S(2)}) collective-permute-start(f32[16,128,128]{2,1,0:T(8,128)} %multiply_add_fusion.9), channel_id=1, source_target_pairs={{0,4},{1,5},{2,6},{3,7},{4,8},{5,9},{6,10},{7,11},{8,12},{9,13},{1... | collective-permute-start | bytes 3145736 | tf_op jit(solution)/shard_map/ppermute | solution.py:19
  103.8 15.3 %collective-permute-start.5 = (s32[]{:T(128)}, s32[]{:T(128)}, u32[]{:S(2)}, u32[]{:S(2)}) collective-permute-start(s32[]{:T(128)} %max.9), channel_id=1, source_target_pairs={{0,2},{1,3},{2,4},{3,5},{4,6},{5,7},{6,8},{7,9},{8,10},{9,11},{10,... | collective-permute-start | bytes 20 | tf_op jit(solution)/shard_map/ppermute | solution.py:19
  119.7 2.7 %multiply_add_fusion.1 = f32[16,128,128]{2,1,0:T(8,128)} fusion(f32[16,128,128]{2,1,0:T(8,128)} %multiply_add_fusion.2, f32[16,128,128]{2,1,0:T(8,128)} %collective-permute-done.11, f32[]{:T(128)S(6)} %convert_element_type.82), kind=kLoop, calls=%fused_computation.30 | loop fusion | flops 524288 | bytes 3145732 | tf_op jit(solution)/shard_map/add | solution.py:67
  122.3 5.6 %collective-permute-start.12 = (f32[16,128,128]{2,1,0:T(8,128)}, f32[16,128,128]{2,1,0:T(8,128)}, u32[]{:S(2)}, u32[]{:S(2)}) collective-permute-start(f32[16,128,128]{2,1,0:T(8,128)} %multiply_add_fusion.1), channel_id=1, source_target_pairs={{0,4},{1,5},{2,6},{3,7},{4,8},{5,9},{6,10},{7,11},{8,12},{9,13},{1... | collective-permute-start | bytes 3145736 | tf_op jit(solution)/shard_map/ppermute | solution.py:19
  127.9 13.7 %collective-permute-done.6 = f32[16,128,128]{2,1,0:T(8,128)} collective-permute-done((f32[16,128,128]{2,1,0:T(8,128)}, f32[16,128,128]{2,1,0:T(8,128)}, u32[]{:S(2)}, u32[]{:S(2)}) %collective-permute-start.6) | collective-permute-done | bytes 1048608 | tf_op jit(solution)/shard_map/ppermute | solution.py:19
  141.6 2.7 %multiply_add_fusion.8 = f32[16,128,128]{2,1,0:T(8,128)} fusion(f32[16,128,128]{2,1,0:T(8,128)} %multiply_add_fusion.9, f32[16,128,128]{2,1,0:T(8,128)} %collective-permute-done.6, f32[]{:T(128)S(6)} %convert_element_type.83), kind=kLoop, calls=%fused_computation.49 | loop fusion | flops 524288 | bytes 3145732 | tf_op jit(solution)/shard_map/add | solution.py:66
  144.3 20.7 %collective-permute-start.8 = (f32[16,128,128]{2,1,0:T(8,128)}, f32[16,128,128]{2,1,0:T(8,128)}, u32[]{:S(2)}, u32[]{:S(2)}) collective-permute-start(f32[16,128,128]{2,1,0:T(8,128)} %multiply_add_fusion.8), channel_id=1, source_target_pairs={{0,8},{1,9},{2,10},{3,11},{4,12},{5,13},{6,14},{7,15},{8,16},{9,17... | collective-permute-start | bytes 3145736 | tf_op jit(solution)/shard_map/ppermute | solution.py:19
  166.8 3.3 %fusion.28 = f32[16,128,128]{1,2,0:T(8,128)} fusion(f32[16,128,128]{2,1,0:T(8,128)S(1)} %convolution_multiply_fusion.8, f32[16,128,128]{1,2,0:T(8,128)S(1)} %bitcast.67, f32[16,128]{1,0:T(8,128)S(1)} %add_rsqrt_fusion), kind=kOutput, calls=%fused_computation.66 | convolution fusion | flops 402915328 | bytes 3153920 | tf_op jit(solution)/shard_map/hts,hsi->hti/dot_general | solution.py:40
  170.1 6.2 %collective-permute-start.7 = (s32[]{:T(128)}, s32[]{:T(128)}, u32[]{:S(2)}, u32[]{:S(2)}) collective-permute-start(s32[]{:T(128)} %max.10), channel_id=1, source_target_pairs={{0,4},{1,5},{2,6},{3,7},{4,8},{5,9},{6,10},{7,11},{8,12},{9,13},{1... | collective-permute-start | bytes 20 | tf_op jit(solution)/shard_map/ppermute | solution.py:19
  178.7 28.7 %collective-permute-start.13 = (f32[16,128,128]{2,1,0:T(8,128)S(1)}, f32[16,128,128]{2,1,0:T(8,128)S(1)}, u32[]{:S(2)}, u32[]{:S(2)}) collective-permute-start(f32[16,128,128]{2,1,0:T(8,128)S(1)} %multiply_add_fusion), channel_id=1, source_target_pairs={{0,8},{1,9},{2,10},{3,11},{4,12},{5,13},{6,14},{7,15},{8,16},{9,17... | collective-permute-start | bytes 3145736 | tf_op jit(solution)/shard_map/ppermute | solution.py:19
  209.1 2.7 %multiply_reduce_fusion.6 = (f32[16,128]{1,0:T(8,128)S(1)}, f32[16,128]{1,0:T(8,128)S(1)}, f32[16,128,128]{1,2,0:T(8,128)S(1)}) fusion(f32[16,128]{1,0:T(8,128)S(1)} %add_rsqrt_fusion.1, f32[128,2048]{0,1:T(8,128)S(1)} %copy.29, f32[16,128,128]{1,2,0:T(8,128)S(1)} %bitcast.76, f32[16,128,128]{1,2,0:T(8,128)} %fusion.28, f32[128]{0:T(128)S(1)} %get-tuple-element.11, ...), kind=kOutput, calls=%fused_computation.47 | convolution fusion | flops 405270528 | bytes 5267968 | tf_op jit(solution)/shard_map/htj,hij->hti/dot_general | solution.py:37
  226.9 2.3 fusion.25
  (72 shorter events, 37.7 us)
Async XLA Ops:
  3.8 99.6 %copy-start.1 = (bf16[128,2048]{1,0:T(8,128)(2,1)S(1)}, bf16[128,2048]{1,0:T(8,128)(2,1)}, u32[]{:S(2)}) copy-start(bf16[128,2048]{1,0:T(8,128)(2,1)} %param.6) | copy-start | bytes 1572868
  9.0 12.5 %collective-permute-start = (f32[16,128,128]{2,1,0:T(8,128)}, f32[16,128,128]{2,1,0:T(8,128)S(1)}, u32[]{:S(2)}, u32[]{:S(2)}) collective-permute-start(f32[16,128,128]{2,1,0:T(8,128)} %fusion), channel_id=1, source_target_pairs={{0,1},{1,2},{2,3},{3,4},{4,5},{5,6},{6,7},{7,8},{8,9},{9,10},{10,1... | collective-permute-start | bytes 3145736 | tf_op jit(solution)/shard_map/ppermute | solution.py:19
  16.0 18.4 %collective-permute-start.9 = (f32[16,128,128]{2,1,0:T(8,128)}, f32[16,128,128]{2,1,0:T(8,128)}, u32[]{:S(2)}, u32[]{:S(2)}) collective-permute-start(f32[16,128,128]{2,1,0:T(8,128)} %fusion.15), channel_id=1, source_target_pairs={{0,1},{1,2},{2,3},{3,4},{4,5},{5,6},{6,7},{7,8},{8,9},{9,10},{10,1... | collective-permute-start | bytes 3145736 | tf_op jit(solution)/shard_map/ppermute | solution.py:19
  21.4 30.5 %copy-start = (f32[16,128,128]{2,1,0:T(8,128)}, f32[16,128,128]{2,1,0:T(8,128)S(1)}, u32[]{:S(2)}) copy-start(f32[16,128,128]{2,1,0:T(8,128)S(1)} %collective-permute-done) | copy-start | bytes 3145732
  21.4 30.5 %collective-permute-start.2 = (f32[16,128,128]{2,1,0:T(8,128)S(1)}, f32[16,128,128]{2,1,0:T(8,128)}, u32[]{:S(2)}, u32[]{:S(2)}) collective-permute-start(f32[16,128,128]{2,1,0:T(8,128)S(1)} %collective-permute-done), channel_id=1, source_target_pairs={{0,1},{1,2},{2,3},{3,4},{4,5},{5,6},{6,7},{7,8},{8,9},{9,10},{10,1... | collective-permute-start | bytes 3145736 | tf_op jit(solution)/shard_map/ppermute | solution.py:19
  29.5 4.2 %collective-permute-start.1 = (s32[]{:T(128)}, s32[]{:T(128)}, u32[]{:S(2)}, u32[]{:S(2)}) collective-permute-start(s32[]{:T(128)} %convert_element_type.80), channel_id=1, source_target_pairs={{0,1},{1,2},{2,3},{3,4},{4,5},{5,6},{6,7},{7,8},{8,9},{9,10},{10,1... | collective-permute-start | bytes 20 | tf_op jit(solution)/shard_map/ppermute | solution.py:19
  34.4 30.1 %collective-permute-start.10 = (f32[16,128,128]{2,1,0:T(8,128)}, f32[16,128,128]{2,1,0:T(8,128)}, u32[]{:S(2)}, u32[]{:S(2)}) collective-permute-start(f32[16,128,128]{2,1,0:T(8,128)} %collective-permute-done.9), channel_id=1, source_target_pairs={{0,1},{1,2},{2,3},{3,4},{4,5},{5,6},{6,7},{7,8},{8,9},{9,10},{10,1... | collective-permute-start | bytes 3145736 | tf_op jit(solution)/shard_map/ppermute | solution.py:19
  53.6 43.6 %collective-permute-start.4 = (f32[16,128,128]{2,1,0:T(8,128)S(1)}, f32[16,128,128]{2,1,0:T(8,128)}, u32[]{:S(2)}, u32[]{:S(2)}) collective-permute-start(f32[16,128,128]{2,1,0:T(8,128)S(1)} %multiply_add_fusion.10), channel_id=1, source_target_pairs={{0,2},{1,3},{2,4},{3,5},{4,6},{5,7},{6,8},{7,9},{8,10},{9,11},{10,... | collective-permute-start | bytes 3145736 | tf_op jit(solution)/shard_map/ppermute | solution.py:19
  58.1 5.3 %collective-permute-start.3 = (s32[]{:T(128)}, s32[]{:T(128)}, u32[]{:S(2)}, u32[]{:S(2)}) collective-permute-start(s32[]{:T(128)} %collective-permute-done.1), channel_id=1, source_target_pairs={{0,1},{1,2},{2,3},{3,4},{4,5},{5,6},{6,7},{7,8},{8,9},{9,10},{10,1... | collective-permute-start | bytes 20 | tf_op jit(solution)/shard_map/ppermute | solution.py:19
  67.2 52.5 %collective-permute-start.11 = (f32[16,128,128]{2,1,0:T(8,128)}, f32[16,128,128]{2,1,0:T(8,128)}, u32[]{:S(2)}, u32[]{:S(2)}) collective-permute-start(f32[16,128,128]{2,1,0:T(8,128)} %multiply_add_fusion.2), channel_id=1, source_target_pairs={{0,2},{1,3},{2,4},{3,5},{4,6},{5,7},{6,8},{7,9},{8,10},{9,11},{10,... | collective-permute-start | bytes 3145736 | tf_op jit(solution)/shard_map/ppermute | solution.py:19
  99.6 42.0 %collective-permute-start.6 = (f32[16,128,128]{2,1,0:T(8,128)}, f32[16,128,128]{2,1,0:T(8,128)}, u32[]{:S(2)}, u32[]{:S(2)}) collective-permute-start(f32[16,128,128]{2,1,0:T(8,128)} %multiply_add_fusion.9), channel_id=1, source_target_pairs={{0,4},{1,5},{2,6},{3,7},{4,8},{5,9},{6,10},{7,11},{8,12},{9,13},{1... | collective-permute-start | bytes 3145736 | tf_op jit(solution)/shard_map/ppermute | solution.py:19
  103.8 15.3 %collective-permute-start.5 = (s32[]{:T(128)}, s32[]{:T(128)}, u32[]{:S(2)}, u32[]{:S(2)}) collective-permute-start(s32[]{:T(128)} %max.9), channel_id=1, source_target_pairs={{0,2},{1,3},{2,4},{3,5},{4,6},{5,7},{6,8},{7,9},{8,10},{9,11},{10,... | collective-permute-start | bytes 20 | tf_op jit(solution)/shard_map/ppermute | solution.py:19
  122.3 54.7 %collective-permute-start.12 = (f32[16,128,128]{2,1,0:T(8,128)}, f32[16,128,128]{2,1,0:T(8,128)}, u32[]{:S(2)}, u32[]{:S(2)}) collective-permute-start(f32[16,128,128]{2,1,0:T(8,128)} %multiply_add_fusion.1), channel_id=1, source_target_pairs={{0,4},{1,5},{2,6},{3,7},{4,8},{5,9},{6,10},{7,11},{8,12},{9,13},{1... | collective-permute-start | bytes 3145736 | tf_op jit(solution)/shard_map/ppermute | solution.py:19
  144.3 63.2 %collective-permute-start.8 = (f32[16,128,128]{2,1,0:T(8,128)}, f32[16,128,128]{2,1,0:T(8,128)}, u32[]{:S(2)}, u32[]{:S(2)}) collective-permute-start(f32[16,128,128]{2,1,0:T(8,128)} %multiply_add_fusion.8), channel_id=1, source_target_pairs={{0,8},{1,9},{2,10},{3,11},{4,12},{5,13},{6,14},{7,15},{8,16},{9,17... | collective-permute-start | bytes 3145736 | tf_op jit(solution)/shard_map/ppermute | solution.py:19
  170.1 6.2 %collective-permute-start.7 = (s32[]{:T(128)}, s32[]{:T(128)}, u32[]{:S(2)}, u32[]{:S(2)}) collective-permute-start(s32[]{:T(128)} %max.10), channel_id=1, source_target_pairs={{0,4},{1,5},{2,6},{3,7},{4,8},{5,9},{6,10},{7,11},{8,12},{9,13},{1... | collective-permute-start | bytes 20 | tf_op jit(solution)/shard_map/ppermute | solution.py:19
  178.7 55.6 %collective-permute-start.13 = (f32[16,128,128]{2,1,0:T(8,128)S(1)}, f32[16,128,128]{2,1,0:T(8,128)S(1)}, u32[]{:S(2)}, u32[]{:S(2)}) collective-permute-start(f32[16,128,128]{2,1,0:T(8,128)S(1)} %multiply_add_fusion), channel_id=1, source_target_pairs={{0,8},{1,9},{2,10},{3,11},{4,12},{5,13},{6,14},{7,15},{8,16},{9,17... | collective-permute-start | bytes 3145736 | tf_op jit(solution)/shard_map/ppermute | solution.py:19
  230.4 5.1 %copy-start.2 = (f32[128]{0:T(128)S(1)}, f32[128]{0:T(128)}, u32[]{:S(2)}) copy-start(f32[128]{0:T(128)} %param.10) | copy-start | bytes 1540
  230.5 5.3 %slice-start = ((s8[8388608]{0:T(1024)(128)(4,1)}), s8[4194304]{0:T(1024)(128)(4,1)S(1)}, s32[]{:S(2)}) async-start(s8[8388608]{0:T(1024)(128)(4,1)} %bitcast.77), calls=%async_computation | async-start | bytes 8388608
  233.0 2.8 %slice-start.1 = ((s8[8388608]{0:T(1024)(128)(4,1)}), s8[4194304]{0:T(1024)(128)(4,1)S(1)}, s32[]{:S(2)}) async-start(s8[8388608]{0:T(1024)(128)(4,1)} %bitcast.77), calls=%async_computation.1 | async-start | bytes 8388608
where the time goes:
time: 239 us; the launch traced here: 238 us
  starting transfers between devices  156 us (65%)
  matrix products  37.6 us (16%)
  other arithmetic  20.5 us (9%)
  waiting for transfers between devices  14.4 us (6%)
  between operations  4.9 us (2%)
  local copies, waits for them, and re-layouts  4.1 us (2%)
    ppermute x14, starting transfers between devices, shifted(): return lax.ppermute(block, axis, route)  156 us
    ppermute x14, waiting for transfers between devices, shifted(): return lax.ppermute(block, axis, route)  14.4 us
    dot_general x5, matrix products, apply_state(): jnp.einsum('hts,hsi->hti', scores, target, precision=highest)  11.3 us
    dot_general x5, matrix products, apply_state(): jnp.einsum('htj,hsj->hts', vector, key_block, precision=highest)  9.39 us
    add x4, other arithmetic, combine_states(): latter[0] + carry_on * earlier[0]  8.4 us
    dot_general x5, matrix products, apply_state(): jnp.einsum('htj,hij->hti', vector, prefix_state, precision=highest)  8.28 us
    add x3, other arithmetic, combine_states(): latter[1] + carry_on * earlier[1]  6.98 us
  transfers between devices with their start and end apart: 14, of which 2 were waited for; matrix products, arithmetic and copies ran while one was open for 21% of the time, Pallas kernels for 0%

commit v1 on v0

--- a/solution.py
+++ b/solution.py
@@ -1,3 +1,5 @@
+import math
+
 import jax
 import jax.numpy as jnp
 from jax import lax
@@ -5,7 +7,7 @@
 
 HEAD_DIM = 128
 ITERS = 4
-SPAN = 15
+GROUP = 16
 
 
 epsilon = 1e-06
@@ -60,15 +62,6 @@
     return apply_state(solution, cross, carried, mask, key_block, value_block)
 
 
-def combine_states(earlier, latter):
-    carry_on = (1 - latter[2]).astype(jnp.float32)
-    return (
-        latter[0] + carry_on * earlier[0],
-        latter[1] + carry_on * earlier[1],
-        jnp.maximum(earlier[2], latter[2]),
-    )
-
-
 def on_device(query_rows, key_rows, value_rows, doc_lengths, norm_gain, out_weight):
     tokens_here = query_rows.shape[0]
     heads_here = query_rows.shape[1] // HEAD_DIM
@@ -85,7 +78,6 @@
     doc_ids = document_ids(doc_lengths, positions)
     previous = document_ids(doc_lengths, positions[:1] - 1)[0]
     carried = (doc_ids == previous).astype(jnp.float32)
-    restart = (doc_ids[-1] != previous).astype(jnp.int32)
     tail_mask = (doc_ids == doc_ids[-1]).astype(jnp.float32)
     tail_gram = jnp.einsum(
         "hsi,hsj->hij", keys_here * tail_mask[None, :, None], keys_here, precision=highest
@@ -93,11 +85,29 @@
     tail_cross = jnp.einsum(
         "hsi,hsj->hij", values * tail_mask[None, :, None], keys_here, precision=highest
     )
-    partial_value = shifted((tail_gram, tail_cross, restart), "seq", 1)
-    for degree in range(SPAN.bit_length()):
-        earlier = shifted((partial_value[0], partial_value[1], partial_value[2]), "seq", 2**degree)
-        partial_value = combine_states(earlier, partial_value)
-    gram, cross, unused = partial_value
+    size = lax.axis_size("seq")
+    group = math.gcd(size, GROUP)
+    groups = [list(range(first, first + group)) for first in range(0, size, group)]
+    first = shard_index // group * group
+    bounds = (first + jnp.arange(group + 1, dtype=jnp.int32)) * tokens_here - 1
+    before = document_ids(doc_lengths, bounds)
+    goes_on = (before[1:] == before[:-1]).astype(jnp.float32)
+    tails = jnp.concatenate([tail_gram, tail_cross], axis=1)
+    pieces = tails.reshape(group, heads_here * 2 * HEAD_DIM // group, HEAD_DIM)
+    pieces = lax.all_to_all(pieces, "seq", 0, 0, axis_index_groups=groups, tiled=True)
+    running = jnp.zeros_like(pieces[0])
+    through = jnp.float32(1)
+    prefixes, throughs = [], []
+    for j in range(group):
+        prefixes.append(running)
+        throughs.append(through)
+        running = pieces[j] + goes_on[j] * running
+        through = through * goes_on[j]
+    carry = shifted(running, "seq", group)
+    prefixes = jnp.stack([p + t * carry for p, t in zip(prefixes, throughs)])
+    prefixes = lax.all_to_all(prefixes, "seq", 0, 0, axis_index_groups=groups, tiled=True)
+    states = prefixes.reshape(heads_here, 2 * HEAD_DIM, HEAD_DIM)
+    gram, cross = states[:, :HEAD_DIM], states[:, HEAD_DIM:]
     causal = offsets[None, :] <= offsets[:, None]
     mask = ((doc_ids[:, None] == doc_ids[None, :]) & causal).astype(jnp.float32)
     mixed_heads = solve_block(queries, keys_here, values, gram, cross, carried, mask)

time: 239 us -> 161 us (0.67)
  starting transfers between devices: 156 us -> 16 us
  waiting for transfers between devices: 14.4 us -> 54.6 us
  other arithmetic: 20.5 us -> 35.8 us
  between operations: 4.9 us -> 10.9 us
    ppermute x14 -> x1, starting transfers between devices: 156 us -> 4.49 us  [shifted(): return lax.ppermute(block, axis, route)]
    all_to_all x0 -> x2, waiting for transfers between devices: none -> 54.6 us  [the longest x1 27.7 us: on_device(): lax.all_to_all(pieces, 'seq', 0, 0, axis_index_groups=groups, tiled=True)]
    unnamed x1 -> x15, other arithmetic: 0.01 us -> 17.3 us
    ppermute x14 -> x1, waiting for transfers between devices: 14.4 us -> 0.01 us  [shifted(): return lax.ppermute(block, axis, route)]
    all_to_all x0 -> x2, starting transfers between devices: none -> 11.5 us  [the longest x1 6.29 us: on_device(): lax.all_to_all(pieces, 'seq', 0, 0, axis_index_groups=groups, tiled=True)]
    add x7 -> x1, other arithmetic: 15.4 us -> 10 us  [on_device(): running = pieces[j] + goes_on[j] * running]
    dot_general x5, matrix products: 8.28 us -> 11.9 us  [apply_state(): jnp.einsum('htj,hij->hti', vector, prefix_state, precision=highest)]
  transfers between devices with their start and end apart: 14 -> 3, of which waited for: 2 -> 2; matrix products, arithmetic and copies ran while one was open for 21% -> 2% of each run, Pallas kernels for 0% -> 0%
where the time goes in v1:
time: 161 us; the launch traced here: 160 us
  waiting for transfers between devices  54.6 us (34%)
  matrix products  38.7 us (24%)
  other arithmetic  35.8 us (22%)
  starting transfers between devices  16 us (10%)
  between operations  10.9 us (7%)
  local copies, waits for them, and re-layouts  4.51 us (3%)
    all_to_all x1, waiting for transfers between devices, on_device(): lax.all_to_all(pieces, 'seq', 0, 0, axis_index_groups=groups, tiled=True)  27.7 us
    all_to_all x1, waiting for transfers between devices, on_device(): lax.all_to_all(prefixes, 'seq', 0, 0, axis_index_groups=groups, tiled=True)  26.9 us
    unnamed x15, other arithmetic  17.3 us
    dot_general x5, matrix products, apply_state(): jnp.einsum('htj,hij->hti', vector, prefix_state, precision=highest)  11.9 us
    dot_general x5, matrix products, apply_state(): jnp.einsum('hts,hsi->hti', scores, target, precision=highest)  10.6 us
    add x1, other arithmetic, on_device(): running = pieces[j] + goes_on[j] * running  10 us
    dot_general x5, matrix products, apply_state(): jnp.einsum('htj,hsj->hts', vector, key_block, precision=highest)  9.6 us
    all_to_all x1, starting transfers between devices, on_device(): lax.all_to_all(pieces, 'seq', 0, 0, axis_index_groups=groups, tiled=True)  6.29 us
  transfers between devices with their start and end apart: 3, of which 2 were waited for; matrix products, arithmetic and copies ran while one was open for 2% of the time, Pallas kernels for 0%

profile of v1, /device:TPU:0, one launch (start us, length us, event | category | flops | bytes accessed | tf_op | source)
XLA Modules:
  0.0 160.5 jit_solution(11114460705381420689)
XLA Ops:
  6.0 2.3 %fusion = f32[16,128,128]{2,1,0:T(8,128)S(1)} fusion(f32[128]{0:T(128)S(1)} %get-tuple-element.20, f32[16,128,128]{1,2,0:T(8,128)S(1)} %bitcast.207, f32[16,128]{1,0:T(8,128)S(1)} %add_rsqrt_fusion), kind=kOutput, calls=%fused_computation.3 | convolution fusion | flops 403439616 | bytes 2105856 | tf_op jit(solution)/shard_map/hsi,hsj->hij/dot_general | solution.py:82
  8.3 2.2 %fusion.9 = f32[16,128,128]{2,1,0:T(8,128)S(1)} fusion(bf16[16,128,128]{1,2,0:T(8,128)(2,1)S(1)} %bitcast.223, f32[128]{0:T(128)S(1)} %get-tuple-element.20, f32[16,128,128]{1,2,0:T(8,128)S(1)} %bitcast.208, f32[16,128]{1,0:T(8,128)S(1)} %add_rsqrt_fusion), kind=kOutput, calls=%fused_computation.42 | convolution fusion | flops 403439616 | bytes 2630144 | tf_op jit(solution)/shard_map/hsi,hsj->hij/dot_general | solution.py:85
  12.0 6.3 %all-to-all-start = ((f32[16,256,128]{2,1,0:T(8,128)}), f32[16,256,128]{2,1,0:T(8,128)S(1)}, u32[]{:S(2)}, u32[]{:S(2)}) async-start(f32[16,256,128]{2,1,0:T(8,128)} %pad_maximum_fusion), calls=%async_computation | async-start | bytes 4194304 | tf_op jit(solution)/shard_map/all_to_all | solution.py:97
  20.0 27.7 %all-to-all-done = f32[16,256,128]{2,1,0:T(8,128)S(1)} async-done(((f32[16,256,128]{2,1,0:T(8,128)}), f32[16,256,128]{2,1,0:T(8,128)S(1)}, u32[]{:S(2)}, u32[]{:S(2)}) %all-to-all-start) | async-done | bytes 2097184 | tf_op jit(solution)/shard_map/all_to_all | solution.py:97
  47.7 10.0 %fusion.37 = (f32[256,128]{1,0:T(8,128)}, f32[256,128]{1,0:T(8,128)S(1)}, f32[256,128]{1,0:T(8,128)S(1)}, f32[256,128]{1,0:T(8,128)}, f32[256,128]{1,0:T(8,128)}...) fusion(f32[16,256,128]{2,1,0:T(8,128)S(1)} %all-to-all-done, f32[]{:T(128)} %bitcast.11, f32[]{:T(128)} %bitcast.13, ...), kind=kLoop, calls=%fused_computation.90 | loop fusion | flops 1015808 | bytes 3145792 | tf_op jit(solution)/shard_map/add | solution.py:104
  57.7 4.5 %collective-permute-start = (f32[256,128]{1,0:T(8,128)}, f32[256,128]{1,0:T(8,128)S(1)}, u32[]{:S(2)}, u32[]{:S(2)}) collective-permute-start(f32[256,128]{1,0:T(8,128)} %get-tuple-element.11), channel_id=1, source_target_pairs={{0,16},{1,17},{2,18},{3,19},{4,20},{5,21},{6,22},{7,23},{8,24},{9,... | collective-permute-start | bytes 393224 | tf_op jit(solution)/shard_map/ppermute | solution.py:21
  74.8 2.1 %bitcast_dynamic-update-slice_fusion.12 = f32[16,256,128]{2,1,0:T(8,128)} fusion(f32[16,256,128]{2,1,0:T(8,128)} %bitcast_dynamic-update-slice_fusion.13, f32[256,128]{1,0:T(8,128)S(1)} %collective-permute-done, f32[]{:T(128)S(6)} %mul.513, f32[256,128]{1,0:T(8,128)} %get-tuple-element.18, f32[]{:T(128)} %bitcast.37, f32[16,256,128]{2,1,0:T(8,128)S(1)} %all-to-all-done), kind=kLoop, calls=%fused_computation.103 | loop fusion | flops 131072 | bytes 524804
  78.6 2.1 %bitcast_dynamic-update-slice_fusion.10 = f32[16,256,128]{2,1,0:T(8,128)} fusion(f32[16,256,128]{2,1,0:T(8,128)} %bitcast_dynamic-update-slice_fusion.11, f32[256,128]{1,0:T(8,128)S(1)} %collective-permute-done, f32[]{:T(128)S(6)} %mul.519, f32[256,128]{1,0:T(8,128)} %get-tuple-element.17, f32[]{:T(128)} %bitcast.33, f32[16,256,128]{2,1,0:T(8,128)S(1)} %all-to-all-done), kind=kLoop, calls=%fused_computation.101 | loop fusion | flops 131072 | bytes 524804
  90.6 5.2 %all-to-all-start.1 = ((f32[16,256,128]{2,1,0:T(8,128)}), f32[16,256,128]{2,1,0:T(8,128)}, u32[]{:S(2)}, u32[]{:S(2)}) async-start(f32[16,256,128]{2,1,0:T(8,128)} %bitcast_dynamic-update-slice_fusion), calls=%async_computation.1 | async-start | bytes 4194304 | tf_op jit(solution)/shard_map/all_to_all | solution.py:108
  96.2 1.9 %convolution_multiply_fusion.8 = f32[16,128,128]{2,1,0:T(8,128)S(1)} fusion(f32[16,128,128]{1,2,0:T(8,128)S(1)} %bitcast.218, f32[128,128]{1,0:T(8,128)S(1)} %fusion.39, f32[16,128]{1,0:T(8,128)S(1)} %add_rsqrt_fusion.1, f32[16,128,128]{1,2,0:T(8,128)S(1)} %bitcast.209, f32[16,128]{1,0:T(8,128)S(1)} %add_rsqrt_fusion), kind=kOutput, calls=%fused_computation.21 | convolution fusion | flops 403439616 | bytes 3227648 | tf_op jit(solution)/shard_map/htj,hsj->hts/dot_general | solution.py:41
  98.1 26.9 %all-to-all-done.1 = f32[16,256,128]{2,1,0:T(8,128)} async-done(((f32[16,256,128]{2,1,0:T(8,128)}), f32[16,256,128]{2,1,0:T(8,128)}, u32[]{:S(2)}, u32[]{:S(2)}) %all-to-all-start.1) | async-done | bytes 2097184 | tf_op jit(solution)/shard_map/all_to_all | solution.py:108
  125.0 2.4 %convolution_multiply_fusion.9 = f32[16,128,128]{1,2,0:T(8,128)S(1)} fusion(f32[16,256,128]{2,1,0:T(8,128)} %all-to-all-done.1, f32[16,128,128]{1,2,0:T(8,128)S(1)} %bitcast.219, f32[128]{0:T(128)S(1)} %get-tuple-element.19, f32[16,128]{1,0:T(8,128)S(1)} %add_rsqrt_fusion.1), kind=kOutput, calls=%fused_computation.22 | convolution fusion | flops 403177472 | bytes 3154432 | tf_op jit(solution)/shard_map/htj,hij->hti/dot_general | solution.py:39
  127.3 2.4 %multiply_reduce_fusion.6 = (f32[16,128]{1,0:T(8,128)S(1)}, f32[16,128]{1,0:T(8,128)S(1)}, f32[16,128,128]{1,2,0:T(8,128)S(1)}) fusion(f32[16,128]{1,0:T(8,128)S(1)} %add_rsqrt_fusion.1, f32[128,2048]{0,1:T(8,128)S(1)} %copy.29, f32[16,128,128]{1,2,0:T(8,128)S(1)} %bitcast.220, f32[16,128,128]{1,2,0:T(8,128)S(1)} %convolution_multiply_fusion.9, ...), kind=kOutput, calls=%fused_computation.41 | convolution fusion | flops 405008384 | bytes 6324224 | tf_op jit(solution)/shard_map/hts,hsi->hti/dot_general | solution.py:42
  130.3 1.9 %convolution_multiply_fusion.6 = f32[16,128,128]{2,1,0:T(8,128)S(1)} fusion(f32[16,128,128]{1,2,0:T(8,128)S(1)} %multiply_add_fusion.3, f32[128,128]{1,0:T(8,128)S(1)} %fusion.39, f32[16,128,128]{1,2,0:T(8,128)S(1)} %bitcast.211, f32[16,128]{1,0:T(8,128)S(1)} %add_rsqrt_fusion), kind=kOutput, calls=%fused_computation.17 | convolution fusion | flops 403177472 | bytes 3219456 | tf_op jit(solution)/shard_map/htj,hsj->hts/dot_general | solution.py:41
  132.2 2.3 %convolution_multiply_fusion.7 = f32[16,128,128]{1,2,0:T(8,128)S(1)} fusion(f32[16,128,128]{1,2,0:T(8,128)S(1)} %multiply_add_fusion.3, f32[16,256,128]{2,1,0:T(8,128)} %all-to-all-done.1, f32[128]{0:T(128)S(1)} %get-tuple-element.19), kind=kOutput, calls=%fused_computation.18 | convolution fusion | flops 402915328 | bytes 3146240 | tf_op jit(solution)/shard_map/htj,hij->hti/dot_general | solution.py:39
  134.5 2.3 %multiply_reduce_fusion.4 = (f32[16,128]{1,0:T(8,128)S(1)}, f32[16,128,128]{1,2,0:T(8,128)S(1)}) fusion(f32[16,128,128]{1,2,0:T(8,128)S(1)} %multiply_add_fusion.3, f32[16,128,128]{1,2,0:T(8,128)S(1)} %convolution_multiply_fusion.7, f32[16,128,128]{2,1,0:T(8,128)S(1)} %convolution_multiply_fusion.6, f32[16,128,128]{1,2,0:T(8,128)S(1)} %bitcast.212, ...), kind=kOutput, calls=%fused_computation.37 | convolution fusion | flops 403961856 | bytes 5259264 | tf_op jit(solution)/shard_map/hts,hsi->hti/dot_general | solution.py:42
  137.8 2.1 %convolution_multiply_fusion.4 = f32[16,128,128]{2,1,0:T(8,128)S(1)} fusion(f32[16,128,128]{1,2,0:T(8,128)S(1)} %multiply_add_fusion.2, f32[128,128]{1,0:T(8,128)S(1)} %fusion.39, f32[16,128,128]{1,2,0:T(8,128)S(1)} %bitcast.213, f32[16,128]{1,0:T(8,128)S(1)} %add_rsqrt_fusion), kind=kOutput, calls=%fused_computation.13 | convolution fusion | flops 403177472 | bytes 3219456 | tf_op jit(solution)/shard_map/htj,hsj->hts/dot_general | solution.py:41
  139.8 2.3 %convolution_multiply_fusion.5 = f32[16,128,128]{1,2,0:T(8,128)S(1)} fusion(f32[16,128,128]{1,2,0:T(8,128)S(1)} %multiply_add_fusion.2, f32[16,256,128]{2,1,0:T(8,128)} %all-to-all-done.1, f32[128]{0:T(128)S(1)} %get-tuple-element.19), kind=kOutput, calls=%fused_computation.14 | convolution fusion | flops 402915328 | bytes 3146240 | tf_op jit(solution)/shard_map/htj,hij->hti/dot_general | solution.py:39
  142.1 2.3 %multiply_reduce_fusion.2 = (f32[16,128]{1,0:T(8,128)S(1)}, f32[16,128,128]{1,2,0:T(8,128)S(1)}) fusion(f32[16,128,128]{1,2,0:T(8,128)S(1)} %multiply_add_fusion.2, f32[16,128,128]{1,2,0:T(8,128)S(1)} %convolution_multiply_fusion.5, f32[16,128,128]{2,1,0:T(8,128)S(1)} %convolution_multiply_fusion.4, f32[16,128,128]{1,2,0:T(8,128)S(1)} %bitcast.214, ...), kind=kOutput, calls=%fused_computation.33 | convolution fusion | flops 403961856 | bytes 5259264 | tf_op jit(solution)/shard_map/hts,hsi->hti/dot_general | solution.py:42
  145.0 1.9 %convolution_multiply_fusion.2 = f32[16,128,128]{2,1,0:T(8,128)S(1)} fusion(f32[16,128,128]{1,2,0:T(8,128)S(1)} %multiply_add_fusion.1, f32[128,128]{1,0:T(8,128)S(1)} %fusion.39, f32[16,128,128]{1,2,0:T(8,128)S(1)} %bitcast.215, f32[16,128]{1,0:T(8,128)S(1)} %add_rsqrt_fusion), kind=kOutput, calls=%fused_computation.9 | convolution fusion | flops 403177472 | bytes 3219456 | tf_op jit(solution)/shard_map/htj,hsj->hts/dot_general | solution.py:41
  146.9 2.3 %convolution_multiply_fusion.3 = f32[16,128,128]{1,2,0:T(8,128)S(1)} fusion(f32[16,128,128]{1,2,0:T(8,128)S(1)} %multiply_add_fusion.1, f32[16,256,128]{2,1,0:T(8,128)} %all-to-all-done.1, f32[128]{0:T(128)S(1)} %get-tuple-element.19), kind=kOutput, calls=%fused_computation.10 | convolution fusion | flops 402915328 | bytes 3146240 | tf_op jit(solution)/shard_map/htj,hij->hti/dot_general | solution.py:39
  149.3 2.3 %fusion.5 = f32[16,128]{1,0:T(8,128)S(1)} fusion(f32[16,128,128]{1,2,0:T(8,128)S(1)} %multiply_add_fusion.1, f32[16,128,128]{1,2,0:T(8,128)S(1)} %convolution_multiply_fusion.3, f32[16,128,128]{2,1,0:T(8,128)S(1)} %convolution_multiply_fusion.2, f32[16,128,128]{1,2,0:T(8,128)S(1)} %bitcast.216, f32[16,128]{1,0:T(8,128)S(1)} %add_rsqrt_fusion), kind=kOutput, calls=%fused_computation.23 | convolution fusion | flops 403961856 | bytes 4210688 | tf_op jit(solution)/shard_map/hts,hsi->hti/dot_general | solution.py:42
  154.2 2.6 %convolution_multiply_fusion.1 = f32[16,128,128]{1,2,0:T(8,128)S(1)} fusion(f32[16,128,128]{1,2,0:T(8,128)S(1)} %multiply_add_fusion, f32[16,256,128]{2,1,0:T(8,128)} %all-to-all-done.1, f32[128]{0:T(128)S(1)} %get-tuple-element.19), kind=kOutput, calls=%fused_computation.7 | convolution fusion | flops 402915328 | bytes 3146240 | tf_op jit(solution)/shard_map/htj,hij->hti/dot_general | solution.py:39
  158.4 2.1 %convolution_convert_fusion = bf16[128,2048]{1,0:T(8,128)(2,1)} fusion(bf16[128,2048]{0,1:T(8,128)(2,1)S(1)} %bitcast.225, bf16[2048,2048]{1,0:T(8,128)(2,1)S(1)} %bitcast.222), kind=kOutput, calls=%fused_computation | convolution fusion | flops 1074003968 | bytes 9437184 | tf_op jit(solution)/shard_map/dot_general | solution.py:117
  (77 shorter events, 29.1 us)
Async XLA Ops:
  0.0 4.4 %copy-start.6 = (bf16[128,2048]{1,0:T(8,128)(2,1)S(1)}, bf16[128,2048]{1,0:T(8,128)(2,1)}, u32[]{:S(2)}) copy-start(bf16[128,2048]{1,0:T(8,128)(2,1)} %param.8) | copy-start | bytes 1572868
  4.7 5.8 %copy-start = (bf16[128,2048]{0,1:T(8,128)(2,1)}, bf16[128,2048]{0,1:T(8,128)(2,1)S(1)}, u32[]{:S(2)}) copy-start(bf16[128,2048]{0,1:T(8,128)(2,1)S(1)} %copy.68) | copy-start | bytes 1572868
  12.0 35.6 %all-to-all-start = ((f32[16,256,128]{2,1,0:T(8,128)}), f32[16,256,128]{2,1,0:T(8,128)S(1)}, u32[]{:S(2)}, u32[]{:S(2)}) async-start(f32[16,256,128]{2,1,0:T(8,128)} %pad_maximum_fusion), calls=%async_computation | async-start | bytes 4194304 | tf_op jit(solution)/shard_map/all_to_all | solution.py:97
  57.7 13.6 %collective-permute-start = (f32[256,128]{1,0:T(8,128)}, f32[256,128]{1,0:T(8,128)S(1)}, u32[]{:S(2)}, u32[]{:S(2)}) collective-permute-start(f32[256,128]{1,0:T(8,128)} %get-tuple-element.11), channel_id=1, source_target_pairs={{0,16},{1,17},{2,18},{3,19},{4,20},{5,21},{6,22},{7,23},{8,24},{9,... | collective-permute-start | bytes 393224 | tf_op jit(solution)/shard_map/ppermute | solution.py:21
  71.3 9.5 %copy-start.4 = (f32[256,128]{1,0:T(8,128)S(1)}, f32[256,128]{1,0:T(8,128)}, u32[]{:S(2)}) copy-start(f32[256,128]{1,0:T(8,128)} %get-tuple-element.16) | copy-start | bytes 393220
  71.3 11.4 %copy-start.3 = (f32[256,128]{1,0:T(8,128)S(1)}, f32[256,128]{1,0:T(8,128)}, u32[]{:S(2)}) copy-start(f32[256,128]{1,0:T(8,128)} %get-tuple-element.15) | copy-start | bytes 393220
  71.9 12.7 %copy-start.2 = (f32[256,128]{1,0:T(8,128)S(1)}, f32[256,128]{1,0:T(8,128)}, u32[]{:S(2)}) copy-start(f32[256,128]{1,0:T(8,128)} %get-tuple-element.14) | copy-start | bytes 393220
  90.6 5.2 %copy-start.5 = (bf16[128,2048]{1,0:T(8,128)(2,1)S(1)}, bf16[128,2048]{1,0:T(8,128)(2,1)}, u32[]{:S(2)}) copy-start(bf16[128,2048]{1,0:T(8,128)(2,1)} %param.6) | copy-start | bytes 1572868
  90.6 34.4 %all-to-all-start.1 = ((f32[16,256,128]{2,1,0:T(8,128)}), f32[16,256,128]{2,1,0:T(8,128)}, u32[]{:S(2)}, u32[]{:S(2)}) async-start(f32[16,256,128]{2,1,0:T(8,128)} %bitcast_dynamic-update-slice_fusion), calls=%async_computation.1 | async-start | bytes 4194304 | tf_op jit(solution)/shard_map/all_to_all | solution.py:108
  151.6 6.8 %slice-start = ((s8[8388608]{0:T(1024)(128)(4,1)}), s8[4194304]{0:T(1024)(128)(4,1)S(1)}, s32[]{:S(2)}) async-start(s8[8388608]{0:T(1024)(128)(4,1)} %bitcast.221), calls=%async_computation.2 | async-start | bytes 8388608
  152.3 6.1 %slice-start.1 = ((s8[8388608]{0:T(1024)(128)(4,1)}), s8[4194304]{0:T(1024)(128)(4,1)S(1)}, s32[]{:S(2)}) async-start(s8[8388608]{0:T(1024)(128)(4,1)} %bitcast.221), calls=%async_computation.3 | async-start | bytes 8388608
  154.2 2.7 %copy-start.1 = (bf16[128,2048]{0,1:T(8,128)(2,1)S(1)}, bf16[128,2048]{0,1:T(8,128)(2,1)}, u32[]{:S(2)}) copy-start(bf16[128,2048]{0,1:T(8,128)(2,1)} %copy-done) | copy-start | bytes 1572868
  156.9 1.3 copy-start.7
